TPU v7x, 32 devices: a whole 2x2x4 slice. The times are simulated.
32 devices in a mesh: mp: 2 (over core), heads: 8 (over z, y), tok: 2 (over x).
Axes of the slice: x: 2, y: 2, z: 4, core: 2. Of those that a mesh axis runs over, the one named last changes fastest.
Arguments:
- context: bfloat16 [2, 512, 8192], P('mp', None, 'heads'), may hold values from -6 to 6
- out_weight: bfloat16 [2, 8192, 8192], P('mp', 'heads', 'tok'), may hold values from -0.0625 to 0.0625
- skip_states: bfloat16 [2, 512, 8192], P(None, None, 'tok'), may hold values from -6 to 6
- gram_old: float32 [8192, 8192], P('tok', ('mp', 'heads')), may hold values from -1 to 3
- cross_old: float32 [8192, 8192], P('tok', ('mp', 'heads')), may hold values from -30 to 30
- map_old: float32 [8192, 8192], P('tok', ('mp', 'heads')), may hold values from -0.3 to 0.3
Outputs:
- gram_new: float32 [8192, 8192], P('tok', ('mp', 'heads'))
- cross_new: float32 [8192, 8192], P('tok', ('mp', 'heads'))
- map_new: float32 [8192, 8192], P('tok', ('mp', 'heads'))
- residual_new: float32 [8192, 8192], P('tok', ('mp', 'heads'))
All inputs are finite; a program needn't handle non-finite values.
Results may differ from a plain program's by a relative error of at most 0.03.
Values may be sent and summed in bfloat16 or wider, within the bound.
A program may use at most 256 MiB of HBM per device.

v0:
```python
import jax
import jax.numpy as jnp
from jax import lax
from jax.sharding import PartitionSpec as P

decay_keep = 0.75
ridge_weight = 0.1
f32, bf16 = (jnp.float32, jnp.bfloat16)
CHUNKS = 4


def dot(a, b):
    return jnp.dot(a, b, preferred_element_type=f32)


def token_inner(left, right):
    return lax.dot_general(left, right, (((0,), (0,)), ((), ())), preferred_element_type=f32)


def shifted(block, axis, shift):
    n = lax.axis_size(axis)
    return lax.ppermute(block, axis, [(i, (i + shift) % n) for i in range(n)])


def total_over(value, axis):
    n = lax.axis_size(axis)
    if n & n - 1:
        return lax.psum(value, axis)
    bit = 1
    while bit < n:
        value = value + lax.ppermute(value, axis, [(i, i ^ bit) for i in range(n)])
        bit *= 2
    return value


def sum_tok(value):
    n = lax.axis_size("tok")
    half = value.astype(bf16)
    for shift in range(1, n):
        value = value + shifted(half, "tok", shift).astype(f32)
    return value.astype(bf16)


def make_states(context, out_weight, skip_states, width):
    n_tok, n_heads, n_mp = (lax.axis_size(a) for a in ("tok", "heads", "mp"))
    t, h, k = (lax.axis_index(a) for a in ("tok", "heads", "mp"))
    tokens, features = skip_states.shape[1:]
    share = features // n_heads
    part = dot(context[0], out_weight[0]).astype(bf16)
    mine = lax.psum_scatter(part, "heads", scatter_dimension=1, tiled=True)
    skip = lax.dynamic_slice(skip_states, (k, 0, h * share), (1, tokens, share))[0]
    mine = (mine.astype(f32) + skip.astype(f32)).astype(bf16)
    other = lax.ppermute(mine, "mp", [(0, 1), (1, 0)])
    pair = jnp.stack([jnp.where(k == 0, mine, other), jnp.where(k == 0, other, mine)])
    if share == width and n_tok == n_mp == 2:
        away = lax.ppermute(pair, ("mp", "tok"), [(0, 1), (3, 2)])
        columns = jnp.where(k == t, pair, away)
        half = lax.dynamic_slice_in_dim(pair[0], k * (tokens // 2), tokens // 2, 0)
        rows = lax.all_gather(half, "heads", axis=1, tiled=True)
        rows_other = lax.ppermute(rows, "mp", [(0, 1), (1, 0)])
        first = jnp.where(k == 0, rows, rows_other)
        second = jnp.where(k == 0, rows_other, rows)
        source = jnp.concatenate([first, second], 0)
        return (source, columns[0], columns[1])
    both = lax.all_gather(pair, "heads", axis=2, tiled=True)
    whole = lax.all_gather(both, "tok", axis=2, tiled=True)
    columns = lax.dynamic_slice_in_dim(whole, (k * n_heads + h) * width, width, 2)
    return (both[0], columns[0], columns[1])


def per_device(context, out_weight, skip_states, gram_old, cross_old, map_old):
    n_tok = lax.axis_size("tok")
    t = lax.axis_index("tok")
    tokens = context.shape[1]
    height, width = gram_old.shape
    new_weight = (1.0 - decay_keep) / tokens
    step = height // CHUNKS
    cuts = [slice(c * step, (c + 1) * step) for c in range(CHUNKS)]
    map_half = map_old.astype(bf16)
    gram_old_half = gram_old.astype(bf16)
    panels = [
        lax.all_gather(gram_old_half[cut], ("mp", "heads"), axis=1, tiled=True) for cut in cuts
    ]
    maps = [map_half] + [shifted(map_half, "tok", s) for s in range(1, n_tok)]
    source, source_cols, target_cols = make_states(context, out_weight, skip_states, width)
    gram_new = decay_keep * gram_old + new_weight * token_inner(source, source_cols)
    cross_new = decay_keep * cross_old + new_weight * token_inner(source, target_cols)

    def panel_part(panel, s):
        owner = lax.rem(t - s + n_tok, n_tok)
        return lax.dynamic_slice_in_dim(panel, owner * height, height, 1)

    inner_map = sum_tok(dot(source, map_half))
    residuals, halves = ([], [])
    for cut, panel in zip(cuts, panels):
        product = sum((dot(panel_part(panel, s), maps[s]) for s in range(n_tok)))
        low_rank = token_inner(source[:, cut], inner_map)
        residual = (
            cross_new[cut]
            - decay_keep * product
            - new_weight * low_rank
            - ridge_weight * map_old[cut]
        )
        residuals.append(residual)
        halves.append(residual.astype(bf16))
    away = [[shifted(half, "tok", s) for half in halves] for s in range(1, n_tok)]
    inner_residual = sum_tok(sum((dot(source[:, cut], half) for cut, half in zip(cuts, halves))))
    blocks = [jnp.concatenate(halves, 0)] + [jnp.concatenate(a, 0) for a in away]
    applied, squares, mixed = ([], 0.0, 0.0)
    for cut, panel, residual in zip(cuts, panels, residuals):
        product = sum((dot(panel_part(panel, s), blocks[s]) for s in range(n_tok)))
        low_rank = token_inner(source[:, cut], inner_residual)
        value = decay_keep * product + new_weight * low_rank + ridge_weight * residual
        applied.append(value)
        squares = squares + jnp.sum(residual * residual)
        mixed = mixed + jnp.sum(residual * value)
    totals = jnp.stack([squares, mixed])
    for axis in ("mp", "tok", "heads"):
        totals = total_over(totals, axis)
    step_size = totals[0] / totals[1]
    residual = jnp.concatenate(residuals, 0)
    return (
        gram_new,
        cross_new,
        map_old + step_size * residual,
        residual - step_size * jnp.concatenate(applied, 0),
    )


def solution(mesh):
    block = P("tok", ("mp", "heads"))
    placed = (
        P("mp", None, "heads"),
        P("mp", "heads", "tok"),
        P(None, None, "tok"),
        block,
        block,
        block,
    )
    return jax.shard_map(
        per_device, mesh=mesh, in_specs=placed, out_specs=(block,) * 4, check_vma=False
    )
```

profile of v0, /device:TPU:0, one launch (start us, length us, event | category | flops | bytes accessed | tf_op | source)
XLA Modules:
  0.0 842.1 jit_solution(6807376808990272788)
XLA Ops:
  8.4 9.4 %fusion.35 = bf16[512,4096]{1,0:T(8,128)(2,1)} fusion(bf16[1,1024,4096]{2,1,0:T(8,128)(2,1)} %param.7, bf16[1,512,1024]{2,1,0:T(8,128)(2,1)S(1)} %copy-done), kind=kOutput, calls=%fused_computation.49 | convolution fusion | flops 4297064448 | bytes 13631488 | tf_op jit(solution)/shard_map/dot_general | solution.py:13
  17.9 91.3 %reduce-scatter.2.cloned.1.call-done = bf16[512,512]{1,0:T(8,128)(2,1)} async-done(((bf16[512,4096]{1,0:T(8,128)(2,1)}), bf16[512,512]{1,0:T(8,128)(2,1)}) %reduce-scatter.2.cloned.1.call-update) | async-done | bytes 524304 | tf_op jit(solution)/shard_map/reduce_scatter | solution.py:50
  113.3 3.9 convert_element_type.56
  121.1 43.2 %all-gather.6.cloned.1.call-done = bf16[256,4096]{1,0:T(8,128)(2,1)} async-done(((bf16[256,512]{1,0:T(8,128)(2,1)}), bf16[256,4096]{1,0:T(8,128)(2,1)}) %all-gather.6.cloned.1.call-update) | async-done | bytes 2097168 | tf_op jit(solution)/shard_map/all_gather | solution.py:59
  164.4 3.4 collective-permute-start.2
  167.8 6.0 convert_element_type.57
  173.8 11.4 %collective-permute-done.2 = bf16[2,512,512]{2,1,0:T(8,128)(2,1)S(1)} collective-permute-done((bf16[2,512,512]{2,1,0:T(8,128)(2,1)S(1)}, bf16[2,512,512]{2,1,0:T(8,128)(2,1)S(1)}, u32[]{:S(2)}, u32[]{:S(2)}) %collective-permute-start.2) | collective-permute-done | bytes 1048608 | tf_op jit(solution)/shard_map/ppermute | solution.py:56
  185.3 2.6 broadcast_select_fusion.1
  188.0 5.4 fusion.79
  193.4 2.6 collective-permute-start.4
  196.0 5.0 multiply_add_fusion.2
  201.0 4.9 multiply_add_fusion.1
  207.7 73.5 %collective-permute-done.4 = bf16[512,512]{1,0:T(8,128)(2,1)S(1)} collective-permute-done((bf16[512,512]{1,0:T(8,128)(2,1)S(1)}, bf16[512,512]{1,0:T(8,128)(2,1)S(1)}, u32[]{:S(2)}, u32[]{:S(2)}) %collective-permute-start.4) | collective-permute-done | bytes 524320 | tf_op jit(solution)/shard_map/ppermute | solution.py:22
  281.4 14.3 %all-gather.10.cloned.1.call-done = bf16[1024,8192]{1,0:T(8,128)(2,1)} async-done(((bf16[1024,512]{1,0:T(8,128)(2,1)}), bf16[1024,8192]{1,0:T(8,128)(2,1)}) %all-gather.10.cloned.1.call-update) | async-done | bytes 16777232 | tf_op jit(solution)/shard_map/all_gather | solution.py:82
  295.7 8.3 fusion.25
  305.9 6.6 fusion.21
  312.5 5.0 fusion.82
  318.9 107.4 %all-gather.12.cloned.1.call-done = bf16[1024,8192]{1,0:T(8,128)(2,1)} async-done(((bf16[1024,512]{1,0:T(8,128)(2,1)}), bf16[1024,8192]{1,0:T(8,128)(2,1)}) %all-gather.12.cloned.1.call-update) | async-done | bytes 16777232 | tf_op jit(solution)/shard_map/all_gather | solution.py:82
  426.4 8.3 fusion.13
  436.6 6.7 fusion.17
  443.3 5.0 fusion.81
  449.7 107.4 %all-gather.14.cloned.1.call-done = bf16[1024,8192]{1,0:T(8,128)(2,1)} async-done(((bf16[1024,512]{1,0:T(8,128)(2,1)}), bf16[1024,8192]{1,0:T(8,128)(2,1)}) %all-gather.14.cloned.1.call-update) | async-done | bytes 16777232 | tf_op jit(solution)/shard_map/all_gather | solution.py:82
  557.1 8.5 %fusion.5 = f32[1024,512]{1,0:T(8,128)S(1)} fusion(bf16[4096,512]{1,0:T(8,128)(2,1)} %collective-permute-done.3, bf16[1024,8192]{1,0:T(8,128)(2,1)} %all-gather.14.cloned.1.call-done, s32[]{:T(128)S(6)} %select_n.73), kind=kOutput, calls=%fused_computation.10 | convolution fusion | flops 4294967296 | bytes 14680068 | tf_op jit(solution)/shard_map/dot_general | solution.py:13
  567.2 6.7 fusion.9
  574.0 5.3 fusion.80
  580.7 2.9 fusion.85
  583.6 2.9 fusion.86
  586.6 2.9 fusion.87
  589.5 98.3 %all-gather.8.cloned.1.call-done = bf16[1024,8192]{1,0:T(8,128)(2,1)} async-done(((bf16[1024,512]{1,0:T(8,128)(2,1)}), bf16[1024,8192]{1,0:T(8,128)(2,1)}) %all-gather.8.cloned.1.call-update) | async-done | bytes 16777232 | tf_op jit(solution)/shard_map/all_gather | solution.py:82
  687.8 8.3 fusion.29
  697.2 6.6 fusion.33
  703.9 3.6 fusion.83
  710.3 9.2 %fusion.31 = f32[1024,512]{1,0:T(8,128)S(1)} fusion(bf16[1024,8192]{1,0:T(8,128)(2,1)} %all-gather.8.cloned.1.call-done, s32[]{:T(128)S(6)} %select_n.72, bf16[1024,512]{1,0:T(8,128)(2,1)} %get-tuple-element.29, bf16[1024,512]{1,0:T(8,128)(2,1)} %get-tuple-element.31, bf16[1024,512]{1,0:T(8,128)(2,1)} %get-tuple-element.33, ...), kind=kOutput, calls=%fused_computation.36 | convolution fusion | flops 4311744512 | bytes 14680068 | tf_op jit(solution)/shard_map/dot_general | solution.py:13
  719.6 8.8 %fusion.23 = f32[1024,512]{1,0:T(8,128)S(1)} fusion(bf16[1024,8192]{1,0:T(8,128)(2,1)} %all-gather.10.cloned.1.call-done, s32[]{:T(128)S(6)} %select_n.72, bf16[1024,512]{1,0:T(8,128)(2,1)} %get-tuple-element.29, bf16[1024,512]{1,0:T(8,128)(2,1)} %get-tuple-element.31, bf16[1024,512]{1,0:T(8,128)(2,1)} %get-tuple-element.33, ...), kind=kOutput, calls=%fused_computation.28 | convolution fusion | flops 4311744512 | bytes 14680068 | tf_op jit(solution)/shard_map/dot_general | solution.py:13
  728.4 10.0 %fusion.15 = f32[1024,512]{1,0:T(8,128)} fusion(bf16[1024,8192]{1,0:T(8,128)(2,1)} %all-gather.12.cloned.1.call-done, s32[]{:T(128)S(6)} %select_n.72, bf16[1024,512]{1,0:T(8,128)(2,1)} %get-tuple-element.29, bf16[1024,512]{1,0:T(8,128)(2,1)} %get-tuple-element.31, bf16[1024,512]{1,0:T(8,128)(2,1)} %get-tuple-element.33, ...), kind=kOutput, calls=%fused_computation.20 | convolution fusion | flops 4311744512 | bytes 14680068 | tf_op jit(solution)/shard_map/dot_general | solution.py:13
  738.4 10.1 %fusion.7 = f32[1024,512]{1,0:T(8,128)} fusion(bf16[1024,8192]{1,0:T(8,128)(2,1)} %all-gather.14.cloned.1.call-done, s32[]{:T(128)S(6)} %select_n.72, bf16[1024,512]{1,0:T(8,128)(2,1)} %get-tuple-element.29, bf16[1024,512]{1,0:T(8,128)(2,1)} %get-tuple-element.31, bf16[1024,512]{1,0:T(8,128)(2,1)} %get-tuple-element.33, ...), kind=kOutput, calls=%fused_computation.12 | convolution fusion | flops 4311744512 | bytes 14680068 | tf_op jit(solution)/shard_map/dot_general | solution.py:13
  752.7 8.6 %fusion.27 = f32[1024,512]{1,0:T(8,128)S(1)} fusion(bf16[4096,512]{1,0:T(8,128)(2,1)S(1)} %constant_dynamic-update-slice_fusion, bf16[1024,8192]{1,0:T(8,128)(2,1)} %all-gather.8.cloned.1.call-done, s32[]{:T(128)S(6)} %select_n.73), kind=kOutput, calls=%fused_computation.32 | convolution fusion | flops 4294967296 | bytes 14680068 | tf_op jit(solution)/shard_map/dot_general | solution.py:13
  761.4 3.0 multiply_reduce_fusion.7
  764.4 7.1 fusion.19
  771.5 3.2 multiply_reduce_fusion.6
  776.0 8.3 fusion.11
  784.3 3.0 multiply_reduce_fusion.5
  788.0 8.3 fusion.3
  796.3 3.1 multiply_reduce_fusion.4
  808.9 2.1 collective-permute-done.12
  811.0 3.5 collective-permute-done.13
  816.1 2.9 collective-permute-done.14
  820.9 14.1 %fusion = (f32[4096,512]{1,0:T(8,128)}, f32[4096,512]{1,0:T(8,128)}) fusion(f32[1024,512]{1,0:T(8,128)} %get-tuple-element.42, f32[1024,512]{1,0:T(8,128)} %get-tuple-element.41, f32[1024,512]{1,0:T(8,128)} %get-tuple-element.40, f32[1024,512]{1,0:T(8,128)} %get-tuple-element.39, f32[1024,512]{1,0:T(8,128)} %get-tuple-element.30, ...), kind=kLoop, calls=%fused_computation.2 | loop fusion | flops 20971520 | bytes 41943044 | tf_op jit(solution)/shard_map/sub | solution.py:126
  (118 shorter events, 37.9 us)
Async XLA Ops:
  7.2 102.0 %reduce-scatter.2.cloned.1.call-start = ((), (), s32[]{:S(2)}) async-start(), calls=%async_computation.1 | async-start | bytes 4718592 | tf_op jit(solution)/shard_map/reduce_scatter | solution.py:50
  17.8 146.5 %all-gather.6.cloned.1.call-start = ((), (), s32[]{:S(2)}) async-start(), calls=%async_computation.2 | async-start | bytes 2359296 | tf_op jit(solution)/shard_map/all_gather | solution.py:59
  110.5 2.0 collective-permute-start
  113.3 182.4 %all-gather.10.cloned.1.call-start = ((), (), s32[]{:S(2)}) async-start(), calls=%async_computation.4 | async-start | bytes 17825792 | tf_op jit(solution)/shard_map/all_gather | solution.py:82
  119.4 307.0 %all-gather.12.cloned.1.call-start = ((), (), s32[]{:S(2)}) async-start(), calls=%async_computation.5 | async-start | bytes 17825792 | tf_op jit(solution)/shard_map/all_gather | solution.py:82
  119.9 437.1 %all-gather.14.cloned.1.call-start = ((), (), s32[]{:S(2)}) async-start(), calls=%async_computation.6 | async-start | bytes 17825792 | tf_op jit(solution)/shard_map/all_gather | solution.py:82
  120.5 567.2 %all-gather.8.cloned.1.call-start = ((), (), s32[]{:S(2)}) async-start(), calls=%async_computation.3 | async-start | bytes 17825792 | tf_op jit(solution)/shard_map/all_gather | solution.py:82
  164.3 21.0 %collective-permute-start.1 = (bf16[256,4096]{1,0:T(8,128)(2,1)}, bf16[256,4096]{1,0:T(8,128)(2,1)}, u32[]{:S(2)}, u32[]{:S(2)}) collective-permute-start(bf16[256,4096]{1,0:T(8,128)(2,1)} %all-gather.6.cloned.1.call-done), channel_id=1, source_target_pairs={{0,16},{16,0},{1,17},{17,1},{2,18},{18,2},{3,19},{19,3},{4,20},{20... | collective-permute-start | bytes 6291464 | tf_op jit(solution)/shard_map/ppermute | solution.py:60
  164.4 20.8 %collective-permute-start.2 = (bf16[2,512,512]{2,1,0:T(8,128)(2,1)S(1)}, bf16[2,512,512]{2,1,0:T(8,128)(2,1)S(1)}, u32[]{:S(2)}, u32[]{:S(2)}) collective-permute-start(bf16[2,512,512]{2,1,0:T(8,128)(2,1)S(1)} %pad_maximum_fusion.6), channel_id=1, source_target_pairs={{0,1},{17,16},{2,3},{19,18},{4,5},{21,20},{6,7},{23,22},{8,9},{25,... | collective-permute-start | bytes 3145736 | tf_op jit(solution)/shard_map/ppermute | solution.py:56
  173.8 130.2 %collective-permute-start.3 = (bf16[4096,512]{1,0:T(8,128)(2,1)}, bf16[4096,512]{1,0:T(8,128)(2,1)}, u32[]{:S(2)}, u32[]{:S(2)}) collective-permute-start(bf16[4096,512]{1,0:T(8,128)(2,1)} %convert_element_type.57), channel_id=1, source_target_pairs={{0,1},{1,0},{2,3},{3,2},{4,5},{5,4},{6,7},{7,6},{8,9},{9,8},{10,11... | collective-permute-start | bytes 12582920 | tf_op jit(solution)/shard_map/ppermute | solution.py:22
  185.3 10.7 %slice-start = ((s8[8388608]{0:T(1024)(128)(4,1)}), s8[4194304]{0:T(1024)(128)(4,1)S(1)}, s32[]{:S(2)}) async-start(s8[8388608]{0:T(1024)(128)(4,1)} %bitcast.57), calls=%async_computation.7 | async-start | bytes 8388608
  188.0 17.9 %copy-start.2 = (bf16[256,4096]{1,0:T(8,128)(2,1)}, bf16[256,4096]{1,0:T(8,128)(2,1)S(1)}, u32[]{:S(2)}) copy-start(bf16[256,4096]{1,0:T(8,128)(2,1)S(1)} %get-tuple-element.22) | copy-start | bytes 6291460
  188.0 8.0 slice-start.1
  193.4 7.6 slice-start.2
  193.4 7.6 slice-start.3
  193.4 87.8 %collective-permute-start.4 = (bf16[512,512]{1,0:T(8,128)(2,1)S(1)}, bf16[512,512]{1,0:T(8,128)(2,1)S(1)}, u32[]{:S(2)}, u32[]{:S(2)}) collective-permute-start(bf16[512,512]{1,0:T(8,128)(2,1)S(1)} %get-tuple-element.27), channel_id=1, source_target_pairs={{0,1},{1,0},{2,3},{3,2},{4,5},{5,4},{6,7},{7,6},{8,9},{9,8},{10,11... | collective-permute-start | bytes 1572872 | tf_op jit(solution)/shard_map/ppermute | solution.py:22
  295.7 10.2 %copy-start.24 = (bf16[1024,8192]{1,0:T(8,128)(2,1)S(1)}, bf16[1024,8192]{1,0:T(8,128)(2,1)}, u32[]{:S(2)}) copy-start(bf16[1024,8192]{1,0:T(8,128)(2,1)} %all-gather.10.cloned.1.call-done) | copy-start | bytes 50331652
  304.0 8.5 %copy-start.13 = (bf16[512,1024]{1,0:T(8,128)(2,1)S(1)}, bf16[512,1024]{1,0:T(8,128)(2,1)}, u32[]{:S(2)}) copy-start(bf16[512,1024]{1,0:T(8,128)(2,1)} %get-tuple-element.18) | copy-start | bytes 3145732
  317.5 431.3 %collective-permute-start.6 = (bf16[1024,512]{1,0:T(8,128)(2,1)}, bf16[1024,512]{1,0:T(8,128)(2,1)}, u32[]{:S(2)}, u32[]{:S(2)}) collective-permute-start(bf16[1024,512]{1,0:T(8,128)(2,1)} %get-tuple-element.33), channel_id=1, source_target_pairs={{0,1},{1,0},{2,3},{3,2},{4,5},{5,4},{6,7},{7,6},{8,9},{9,8},{10,11... | collective-permute-start | bytes 3145736 | tf_op jit(solution)/shard_map/ppermute | solution.py:22
  426.4 10.2 %copy-start.23 = (bf16[1024,8192]{1,0:T(8,128)(2,1)S(1)}, bf16[1024,8192]{1,0:T(8,128)(2,1)}, u32[]{:S(2)}) copy-start(bf16[1024,8192]{1,0:T(8,128)(2,1)} %all-gather.12.cloned.1.call-done) | copy-start | bytes 50331652
  436.6 6.7 copy-start.10
  448.3 301.8 %collective-permute-start.7 = (bf16[1024,512]{1,0:T(8,128)(2,1)}, bf16[1024,512]{1,0:T(8,128)(2,1)}, u32[]{:S(2)}, u32[]{:S(2)}) collective-permute-start(bf16[1024,512]{1,0:T(8,128)(2,1)} %get-tuple-element.31), channel_id=1, source_target_pairs={{0,1},{1,0},{2,3},{3,2},{4,5},{5,4},{6,7},{7,6},{8,9},{9,8},{10,11... | collective-permute-start | bytes 3145736 | tf_op jit(solution)/shard_map/ppermute | solution.py:22
  557.1 10.2 %copy-start.22 = (bf16[1024,8192]{1,0:T(8,128)(2,1)S(1)}, bf16[1024,8192]{1,0:T(8,128)(2,1)}, u32[]{:S(2)}) copy-start(bf16[1024,8192]{1,0:T(8,128)(2,1)} %all-gather.14.cloned.1.call-done) | copy-start | bytes 50331652
  567.2 6.7 copy-start.8
  574.0 6.7 copy-start.14
  574.0 9.7 %copy-start.11 = (bf16[512,1024]{1,0:T(8,128)(2,1)S(1)}, bf16[512,1024]{1,0:T(8,128)(2,1)}, u32[]{:S(2)}) copy-start(bf16[512,1024]{1,0:T(8,128)(2,1)} %get-tuple-element.19) | copy-start | bytes 3145732
  579.3 172.2 %collective-permute-start.8 = (bf16[1024,512]{1,0:T(8,128)(2,1)}, bf16[1024,512]{1,0:T(8,128)(2,1)}, u32[]{:S(2)}, u32[]{:S(2)}) collective-permute-start(bf16[1024,512]{1,0:T(8,128)(2,1)} %get-tuple-element.29), channel_id=1, source_target_pairs={{0,1},{1,0},{2,3},{3,2},{4,5},{5,4},{6,7},{7,6},{8,9},{9,8},{10,11... | collective-permute-start | bytes 3145736 | tf_op jit(solution)/shard_map/ppermute | solution.py:22
  687.8 9.4 %copy-start.25 = (bf16[1024,8192]{1,0:T(8,128)(2,1)S(1)}, bf16[1024,8192]{1,0:T(8,128)(2,1)}, u32[]{:S(2)}) copy-start(bf16[1024,8192]{1,0:T(8,128)(2,1)} %all-gather.8.cloned.1.call-done) | copy-start | bytes 50331652
  697.2 6.7 copy-start.3
  703.8 5.1 copy-start.18
  707.4 53.9 %copy-start.7 = (f32[1024,512]{1,0:T(8,128)}, f32[1024,512]{1,0:T(8,128)S(1)}, u32[]{:S(2)}) copy-start(f32[1024,512]{1,0:T(8,128)S(1)} %get-tuple-element.36) | copy-start | bytes 6291460
  707.4 41.3 %collective-permute-start.5 = (bf16[1024,512]{1,0:T(8,128)(2,1)S(1)}, bf16[1024,512]{1,0:T(8,128)(2,1)S(1)}, u32[]{:S(2)}, u32[]{:S(2)}) collective-permute-start(bf16[1024,512]{1,0:T(8,128)(2,1)S(1)} %get-tuple-element.35), channel_id=1, source_target_pairs={{0,1},{1,0},{2,3},{3,2},{4,5},{5,4},{6,7},{7,6},{8,9},{9,8},{10,11... | collective-permute-start | bytes 3145736 | tf_op jit(solution)/shard_map/ppermute | solution.py:22
  709.7 38.8 %collective-permute-start.9 = (bf16[512,512]{1,0:T(8,128)(2,1)S(1)}, bf16[512,512]{1,0:T(8,128)(2,1)S(1)}, u32[]{:S(2)}, u32[]{:S(2)}) collective-permute-start(bf16[512,512]{1,0:T(8,128)(2,1)S(1)} %get-tuple-element.37), channel_id=1, source_target_pairs={{0,1},{1,0},{2,3},{3,2},{4,5},{5,4},{6,7},{7,6},{8,9},{9,8},{10,11... | collective-permute-start | bytes 1572872 | tf_op jit(solution)/shard_map/ppermute | solution.py:22
  752.7 11.7 %copy-start.21 = (bf16[4096,512]{1,0:T(8,128)(2,1)}, bf16[4096,512]{1,0:T(8,128)(2,1)S(1)}, u32[]{:S(2)}) copy-start(bf16[4096,512]{1,0:T(8,128)(2,1)S(1)} %constant_dynamic-update-slice_fusion) | copy-start | bytes 12582916
  764.4 7.1 copy-start.4
  764.4 7.1 copy-start.15
  775.9 8.3 copy-start.5
  775.9 8.3 copy-start.12
  776.0 8.3 copy-start.17
  788.0 8.3 copy-start.6
  788.0 8.3 copy-start.9
  788.0 8.3 copy-start.16
  802.6 1.1 collective-permute-start.10
  803.9 3.5 collective-permute-start.11
  807.5 3.5 collective-permute-start.12
  811.0 3.5 collective-permute-start.13
  814.6 4.4 collective-permute-start.14
  820.9 14.1 %copy-start.1 = (bf16[1,512,1024]{2,1,0:T(8,128)(2,1)S(1)}, bf16[1,512,1024]{2,1,0:T(8,128)(2,1)}, u32[]{:S(2)}) copy-start(bf16[1,512,1024]{2,1,0:T(8,128)(2,1)} %param.6) | copy-start | bytes 3145732
  (3 other events, 11.5 us)
Sparse Core Ops, SparseCore 0:
  17.9 91.1 reduce-scatter.1
  113.4 50.8 all-gather.5
  167.1 128.5 all-gather.9
  297.8 128.5 all-gather.11
  428.5 128.5 all-gather.13
  559.2 128.5 all-gather.7
where the time goes:
time: 848 us; the launch traced here: 842 us
  waiting for transfers between devices  562 us (66%)
  matrix products  196 us (23%)
  other arithmetic  30.7 us (4%)
  between operations  21.2 us (2%)
  starting transfers between devices  17.1 us (2%)
  local copies, waits for them, and re-layouts  15.3 us (2%)
    all_gather x4, waiting for transfers between devices, per_device(): lax.all_gather(gram_old_half[cut], ('mp', 'heads'), axis=1, tiled=True)  327 us
    dot_general x22, matrix products, dot(): return jnp.dot(a, b, preferred_element_type=f32)  155 us
    reduce_scatter x1, waiting for transfers between devices, make_states(): mine = lax.psum_scatter(part, 'heads', scatter_dimension=1, tiled=True)  91.3 us
    ppermute x7, waiting for transfers between devices, shifted(): return lax.ppermute(block, axis, [(i, (i + shift) % n) for i in range(n)])  73.5 us
    all_gather x1, waiting for transfers between devices, make_states(): rows = lax.all_gather(half, 'heads', axis=1, tiled=True)  43.2 us
    dot_general x10, matrix products, token_inner(): lax.dot_general(left, right, (((0,), (0,)), ((), ())), preferred_element_...  41.2 us
  transfers between devices with their start and end apart: 21, of which 14 were waited for; matrix products, arithmetic and copies ran while one was open for 19% of the time, Pallas kernels for 0%

commit v1 on v0

--- a/solution.py
+++ b/solution.py
@@ -56,7 +56,14 @@
         away = lax.ppermute(pair, ("mp", "tok"), [(0, 1), (3, 2)])
         columns = jnp.where(k == t, pair, away)
         half = lax.dynamic_slice_in_dim(pair[0], k * (tokens // 2), tokens // 2, 0)
-        rows = lax.all_gather(half, "heads", axis=1, tiled=True)
+        ring = [half]
+        for hop in range(7):
+            ring.append(lax.ppermute(ring[-1], "heads", [(dev, (dev + 1) % 8) for dev in range(8)]))
+        rows = jnp.roll(
+            jnp.concatenate(ring[::-1], axis=1),
+            (lax.axis_index("heads") + 1) * ring[0].shape[1],
+            axis=1,
+        )
         rows_other = lax.ppermute(rows, "mp", [(0, 1), (1, 0)])
         first = jnp.where(k == 0, rows, rows_other)
         second = jnp.where(k == 0, rows_other, rows)

time: 848 us -> 763 us (0.90)
  waiting for transfers between devices: 562 us -> 468 us
    all_gather x4, waiting for transfers between devices: 327 us -> 100 us  [per_device(): lax.all_gather(gram_old_half[cut], ('mp', 'heads'), axis=1, tiled=True)]
    ppermute x0 -> x7, waiting for transfers between devices: none -> 110 us  [make_states(): lax.ppermute(ring[-1], 'heads', [(dev, (dev + 1) % 8) for dev in range(8)])]
    reduce_scatter x1, waiting for transfers between devices: 91.3 us -> 160 us  [make_states(): mine = lax.psum_scatter(part, 'heads', scatter_dimension=1, tiled=True)]
    all_gather x1 -> x0, waiting for transfers between devices: 43.2 us -> none  [make_states(): rows = lax.all_gather(half, 'heads', axis=1, tiled=True)]
  transfers between devices with their start and end apart: 21 -> 27, of which waited for: 14 -> 18; matrix products, arithmetic and copies ran while one was open for 19% -> 22% of each run, Pallas kernels for 0% -> 0%
where the time goes in v1:
time: 763 us; the launch traced here: 756 us
  waiting for transfers between devices  468 us (61%)
  matrix products  196 us (26%)
  other arithmetic  32.6 us (4%)
  between operations  22.8 us (3%)
  starting transfers between devices  21.1 us (3%)
  local copies, waits for them, and re-layouts  15.8 us (2%)
    reduce_scatter x1, waiting for transfers between devices, make_states(): mine = lax.psum_scatter(part, 'heads', scatter_dimension=1, tiled=True)  160 us
    dot_general x22, matrix products, dot(): return jnp.dot(a, b, preferred_element_type=f32)  155 us
    ppermute x7, waiting for transfers between devices, make_states(): lax.ppermute(ring[-1], 'heads', [(dev, (dev + 1) % 8) for dev in range(8)])  110 us
    all_gather x4, waiting for transfers between devices, per_device(): lax.all_gather(gram_old_half[cut], ('mp', 'heads'), axis=1, tiled=True)  100 us
    ppermute x7, waiting for transfers between devices, shifted(): return lax.ppermute(block, axis, [(i, (i + shift) % n) for i in range(n)])  72.1 us
    dot_general x10, matrix products, token_inner(): lax.dot_general(left, right, (((0,), (0,)), ((), ())), preferred_element_...  41.3 us
  transfers between devices with their start and end apart: 27, of which 18 were waited for; matrix products, arithmetic and copies ran while one was open for 22% of the time, Pallas kernels for 0%

profile of v1, /device:TPU:0, one launch (start us, length us, event | category | flops | bytes accessed | tf_op | source)
XLA Modules:
  0.0 755.9 jit_solution(13386755793787375833)
XLA Ops:
  9.2 9.4 %fusion.35 = bf16[512,4096]{1,0:T(8,128)(2,1)} fusion(bf16[1,1024,4096]{2,1,0:T(8,128)(2,1)} %param.7, bf16[1,512,1024]{2,1,0:T(8,128)(2,1)S(1)} %copy-done), kind=kOutput, calls=%fused_computation.49 | convolution fusion | flops 4297064448 | bytes 13631488 | tf_op jit(solution)/shard_map/dot_general | solution.py:13
  18.7 3.9 convert_element_type.56
  26.6 160.3 %reduce-scatter.2.cloned.1.call-done = bf16[512,512]{1,0:T(8,128)(2,1)} async-done(((bf16[512,4096]{1,0:T(8,128)(2,1)}), bf16[512,512]{1,0:T(8,128)(2,1)}) %reduce-scatter.2.cloned.1.call-update) | async-done | bytes 524304 | tf_op jit(solution)/shard_map/reduce_scatter | solution.py:50
  191.8 15.0 %collective-permute-done.1 = bf16[256,512]{1,0:T(8,128)(2,1)S(1)} collective-permute-done((bf16[256,512]{1,0:T(8,128)(2,1)S(1)}, bf16[256,512]{1,0:T(8,128)(2,1)S(1)}, u32[]{:S(2)}, u32[]{:S(2)}) %collective-permute-start.1) | collective-permute-done | bytes 262176 | tf_op jit(solution)/shard_map/ppermute | solution.py:61
  206.8 16.9 %collective-permute-done.2 = bf16[256,512]{1,0:T(8,128)(2,1)S(1)} collective-permute-done((bf16[256,512]{1,0:T(8,128)(2,1)S(1)}, bf16[256,512]{1,0:T(8,128)(2,1)S(1)}, u32[]{:S(2)}, u32[]{:S(2)}) %collective-permute-start.2) | collective-permute-done | bytes 262176 | tf_op jit(solution)/shard_map/ppermute | solution.py:61
  223.7 15.4 %collective-permute-done.3 = bf16[256,512]{1,0:T(8,128)(2,1)S(1)} collective-permute-done((bf16[256,512]{1,0:T(8,128)(2,1)S(1)}, bf16[256,512]{1,0:T(8,128)(2,1)S(1)}, u32[]{:S(2)}, u32[]{:S(2)}) %collective-permute-start.3) | collective-permute-done | bytes 262176 | tf_op jit(solution)/shard_map/ppermute | solution.py:61
  239.1 14.2 %collective-permute-done.4 = bf16[256,512]{1,0:T(8,128)(2,1)S(1)} collective-permute-done((bf16[256,512]{1,0:T(8,128)(2,1)S(1)}, bf16[256,512]{1,0:T(8,128)(2,1)S(1)}, u32[]{:S(2)}, u32[]{:S(2)}) %collective-permute-start.4) | collective-permute-done | bytes 262176 | tf_op jit(solution)/shard_map/ppermute | solution.py:61
  253.3 15.7 %collective-permute-done.5 = bf16[256,512]{1,0:T(8,128)(2,1)S(1)} collective-permute-done((bf16[256,512]{1,0:T(8,128)(2,1)S(1)}, bf16[256,512]{1,0:T(8,128)(2,1)S(1)}, u32[]{:S(2)}, u32[]{:S(2)}) %collective-permute-start.5) | collective-permute-done | bytes 262176 | tf_op jit(solution)/shard_map/ppermute | solution.py:61
  269.0 15.7 %collective-permute-done.6 = bf16[256,512]{1,0:T(8,128)(2,1)S(1)} collective-permute-done((bf16[256,512]{1,0:T(8,128)(2,1)S(1)}, bf16[256,512]{1,0:T(8,128)(2,1)S(1)}, u32[]{:S(2)}, u32[]{:S(2)}) %collective-permute-start.6) | collective-permute-done | bytes 262176 | tf_op jit(solution)/shard_map/ppermute | solution.py:61
  284.7 17.6 %collective-permute-done.7 = bf16[256,512]{1,0:T(8,128)(2,1)S(1)} collective-permute-done((bf16[256,512]{1,0:T(8,128)(2,1)S(1)}, bf16[256,512]{1,0:T(8,128)(2,1)S(1)}, u32[]{:S(2)}, u32[]{:S(2)}) %collective-permute-start.7) | collective-permute-done | bytes 262176 | tf_op jit(solution)/shard_map/ppermute | solution.py:61
  306.1 4.5 collective-permute-start.9
  310.6 6.4 convert_element_type.57
  317.1 9.4 %collective-permute-done.9 = bf16[2,512,512]{2,1,0:T(8,128)(2,1)} collective-permute-done((bf16[2,512,512]{2,1,0:T(8,128)(2,1)}, bf16[2,512,512]{2,1,0:T(8,128)(2,1)}, u32[]{:S(2)}, u32[]{:S(2)}) %collective-permute-start.9) | collective-permute-done | bytes 1048608 | tf_op jit(solution)/shard_map/ppermute | solution.py:56
  326.6 3.2 broadcast_select_fusion.1
  329.8 5.3 fusion.79
  335.2 4.4 collective-permute-start.11
  339.6 5.0 multiply_add_fusion.2
  344.6 4.9 multiply_add_fusion.1
  351.2 72.1 %collective-permute-done.11 = bf16[512,512]{1,0:T(8,128)(2,1)S(1)} collective-permute-done((bf16[512,512]{1,0:T(8,128)(2,1)S(1)}, bf16[512,512]{1,0:T(8,128)(2,1)S(1)}, u32[]{:S(2)}, u32[]{:S(2)}) %collective-permute-start.11) | collective-permute-done | bytes 524320 | tf_op jit(solution)/shard_map/ppermute | solution.py:22
  423.5 8.3 %fusion.25 = f32[1024,512]{1,0:T(8,128)S(1)} fusion(bf16[4096,512]{1,0:T(8,128)(2,1)} %convert_element_type.57, bf16[1024,8192]{1,0:T(8,128)(2,1)} %all-gather.7.cloned.1.call-done, s32[]{:T(128)S(6)} %select_n.87), kind=kOutput, calls=%fused_computation.30 | convolution fusion | flops 4294967296 | bytes 14680068 | tf_op jit(solution)/shard_map/dot_general | solution.py:13
  433.0 6.5 fusion.21
  439.5 5.3 fusion.82
  447.2 8.3 %fusion.13 = f32[1024,512]{1,0:T(8,128)S(1)} fusion(bf16[4096,512]{1,0:T(8,128)(2,1)} %collective-permute-done.10, bf16[1024,8192]{1,0:T(8,128)(2,1)} %all-gather.9.cloned.1.call-done, s32[]{:T(128)S(6)} %select_n.88), kind=kOutput, calls=%fused_computation.18 | convolution fusion | flops 4294967296 | bytes 14680068 | tf_op jit(solution)/shard_map/dot_general | solution.py:13
  456.8 6.6 fusion.17
  463.4 5.1 fusion.81
  470.5 8.5 %fusion.5 = f32[1024,512]{1,0:T(8,128)S(1)} fusion(bf16[4096,512]{1,0:T(8,128)(2,1)} %collective-permute-done.10, bf16[1024,8192]{1,0:T(8,128)(2,1)} %all-gather.11.cloned.1.call-done, s32[]{:T(128)S(6)} %select_n.88), kind=kOutput, calls=%fused_computation.10 | convolution fusion | flops 4294967296 | bytes 14680068 | tf_op jit(solution)/shard_map/dot_general | solution.py:13
  480.7 6.7 fusion.9
  487.4 5.3 fusion.80
  497.0 2.9 fusion.86
  499.9 3.0 fusion.87
  502.9 98.0 %all-gather.5.cloned.1.call-done = bf16[1024,8192]{1,0:T(8,128)(2,1)} async-done(((bf16[1024,512]{1,0:T(8,128)(2,1)}), bf16[1024,8192]{1,0:T(8,128)(2,1)}) %all-gather.5.cloned.1.call-update) | async-done | bytes 16777232 | tf_op jit(solution)/shard_map/all_gather | solution.py:89
  601.0 8.3 %fusion.29 = f32[1024,512]{1,0:T(8,128)S(1)} fusion(bf16[4096,512]{1,0:T(8,128)(2,1)} %collective-permute-done.10, bf16[1024,8192]{1,0:T(8,128)(2,1)} %all-gather.5.cloned.1.call-done, s32[]{:T(128)S(6)} %select_n.88), kind=kOutput, calls=%fused_computation.34 | convolution fusion | flops 4294967296 | bytes 14680068 | tf_op jit(solution)/shard_map/dot_general | solution.py:13
  610.4 6.6 fusion.33
  617.1 3.5 fusion.83
  623.5 9.2 %fusion.31 = f32[1024,512]{1,0:T(8,128)S(1)} fusion(bf16[1024,8192]{1,0:T(8,128)(2,1)} %all-gather.5.cloned.1.call-done, s32[]{:T(128)S(6)} %select_n.87, bf16[1024,512]{1,0:T(8,128)(2,1)} %get-tuple-element.29, bf16[1024,512]{1,0:T(8,128)(2,1)} %get-tuple-element.31, bf16[1024,512]{1,0:T(8,128)(2,1)} %get-tuple-element.33, ...), kind=kOutput, calls=%fused_computation.36 | convolution fusion | flops 4311744512 | bytes 14680068 | tf_op jit(solution)/shard_map/dot_general | solution.py:13
  632.8 8.8 %fusion.23 = f32[1024,512]{1,0:T(8,128)S(1)} fusion(bf16[1024,8192]{1,0:T(8,128)(2,1)} %all-gather.7.cloned.1.call-done, s32[]{:T(128)S(6)} %select_n.87, bf16[1024,512]{1,0:T(8,128)(2,1)} %get-tuple-element.29, bf16[1024,512]{1,0:T(8,128)(2,1)} %get-tuple-element.31, bf16[1024,512]{1,0:T(8,128)(2,1)} %get-tuple-element.33, ...), kind=kOutput, calls=%fused_computation.28 | convolution fusion | flops 4311744512 | bytes 14680068 | tf_op jit(solution)/shard_map/dot_general | solution.py:13
  641.6 10.2 %fusion.15 = f32[1024,512]{1,0:T(8,128)} fusion(bf16[1024,8192]{1,0:T(8,128)(2,1)} %all-gather.9.cloned.1.call-done, s32[]{:T(128)S(6)} %select_n.87, bf16[1024,512]{1,0:T(8,128)(2,1)} %get-tuple-element.29, bf16[1024,512]{1,0:T(8,128)(2,1)} %get-tuple-element.31, bf16[1024,512]{1,0:T(8,128)(2,1)} %get-tuple-element.33, ...), kind=kOutput, calls=%fused_computation.20 | convolution fusion | flops 4311744512 | bytes 14680068 | tf_op jit(solution)/shard_map/dot_general | solution.py:13
  651.8 10.0 %fusion.7 = f32[1024,512]{1,0:T(8,128)} fusion(bf16[1024,8192]{1,0:T(8,128)(2,1)} %all-gather.11.cloned.1.call-done, s32[]{:T(128)S(6)} %select_n.87, bf16[1024,512]{1,0:T(8,128)(2,1)} %get-tuple-element.29, bf16[1024,512]{1,0:T(8,128)(2,1)} %get-tuple-element.31, bf16[1024,512]{1,0:T(8,128)(2,1)} %get-tuple-element.33, ...), kind=kOutput, calls=%fused_computation.12 | convolution fusion | flops 4311744512 | bytes 14680068 | tf_op jit(solution)/shard_map/dot_general | solution.py:13
  666.1 8.6 %fusion.27 = f32[1024,512]{1,0:T(8,128)S(1)} fusion(bf16[4096,512]{1,0:T(8,128)(2,1)S(1)} %constant_dynamic-update-slice_fusion.16, bf16[1024,8192]{1,0:T(8,128)(2,1)} %all-gather.5.cloned.1.call-done, s32[]{:T(128)S(6)} %select_n.88), kind=kOutput, calls=%fused_computation.32 | convolution fusion | flops 4294967296 | bytes 14680068 | tf_op jit(solution)/shard_map/dot_general | solution.py:13
  674.7 3.1 multiply_reduce_fusion.7
  677.8 7.1 fusion.19
  684.9 3.0 multiply_reduce_fusion.6
  689.1 8.3 %fusion.11 = f32[1024,512]{1,0:T(8,128)S(1)} fusion(bf16[4096,512]{1,0:T(8,128)(2,1)} %copy-done.22, bf16[1024,8192]{1,0:T(8,128)(2,1)} %all-gather.9.cloned.1.call-done, s32[]{:T(128)S(6)} %select_n.88), kind=kOutput, calls=%fused_computation.16 | convolution fusion | flops 4294967296 | bytes 14680068 | tf_op jit(solution)/shard_map/dot_general | solution.py:13
  697.4 3.1 multiply_reduce_fusion.5
  701.2 8.3 %fusion.3 = f32[1024,512]{1,0:T(8,128)S(1)} fusion(bf16[4096,512]{1,0:T(8,128)(2,1)} %copy-done.22, bf16[1024,8192]{1,0:T(8,128)(2,1)} %all-gather.11.cloned.1.call-done, s32[]{:T(128)S(6)} %select_n.88), kind=kOutput, calls=%fused_computation.8 | convolution fusion | flops 4294967296 | bytes 14680068 | tf_op jit(solution)/shard_map/dot_general | solution.py:13
  709.5 3.1 multiply_reduce_fusion.4
  724.1 3.5 collective-permute-done.20
  734.0 14.1 %fusion = (f32[4096,512]{1,0:T(8,128)}, f32[4096,512]{1,0:T(8,128)}) fusion(f32[1024,512]{1,0:T(8,128)} %get-tuple-element.42, f32[1024,512]{1,0:T(8,128)} %get-tuple-element.41, f32[1024,512]{1,0:T(8,128)} %get-tuple-element.40, f32[1024,512]{1,0:T(8,128)} %get-tuple-element.39, f32[1024,512]{1,0:T(8,128)} %get-tuple-element.30, ...), kind=kLoop, calls=%fused_computation.2 | loop fusion | flops 20971520 | bytes 41943044 | tf_op jit(solution)/shard_map/sub | solution.py:133
  (148 shorter events, 50.6 us)
Async XLA Ops:
  8.0 178.9 %reduce-scatter.2.cloned.1.call-start = ((), (), s32[]{:S(2)}) async-start(), calls=%async_computation.1 | async-start | bytes 4718592 | tf_op jit(solution)/shard_map/reduce_scatter | solution.py:50
  18.6 404.9 %all-gather.7.cloned.1.call-start = ((), (), s32[]{:S(2)}) async-start(), calls=%async_computation.3 | async-start | bytes 17825792 | tf_op jit(solution)/shard_map/all_gather | solution.py:89
  24.7 422.4 %all-gather.9.cloned.1.call-start = ((), (), s32[]{:S(2)}) async-start(), calls=%async_computation.4 | async-start | bytes 17825792 | tf_op jit(solution)/shard_map/all_gather | solution.py:89
  25.3 445.2 %all-gather.11.cloned.1.call-start = ((), (), s32[]{:S(2)}) async-start(), calls=%async_computation.5 | async-start | bytes 17825792 | tf_op jit(solution)/shard_map/all_gather | solution.py:89
  25.9 575.1 %all-gather.5.cloned.1.call-start = ((), (), s32[]{:S(2)}) async-start(), calls=%async_computation.2 | async-start | bytes 17825792 | tf_op jit(solution)/shard_map/all_gather | solution.py:89
  188.2 2.0 collective-permute-start
  190.3 16.5 %collective-permute-start.1 = (bf16[256,512]{1,0:T(8,128)(2,1)S(1)}, bf16[256,512]{1,0:T(8,128)(2,1)S(1)}, u32[]{:S(2)}, u32[]{:S(2)}) collective-permute-start(bf16[256,512]{1,0:T(8,128)(2,1)S(1)} %constant_dynamic-slice_fusion.1), channel_id=1, source_target_pairs={{0,2},{2,4},{4,6},{6,8},{8,10},{10,12},{12,14},{14,0},{1,3},{3,5},... | collective-permute-start | bytes 786440 | tf_op jit(solution)/shard_map/ppermute | solution.py:61
  206.8 16.9 %collective-permute-start.2 = (bf16[256,512]{1,0:T(8,128)(2,1)S(1)}, bf16[256,512]{1,0:T(8,128)(2,1)S(1)}, u32[]{:S(2)}, u32[]{:S(2)}) collective-permute-start(bf16[256,512]{1,0:T(8,128)(2,1)S(1)} %collective-permute-done.1), channel_id=1, source_target_pairs={{0,2},{2,4},{4,6},{6,8},{8,10},{10,12},{12,14},{14,0},{1,3},{3,5},... | collective-permute-start | bytes 786440 | tf_op jit(solution)/shard_map/ppermute | solution.py:61
  223.7 15.4 %collective-permute-start.3 = (bf16[256,512]{1,0:T(8,128)(2,1)S(1)}, bf16[256,512]{1,0:T(8,128)(2,1)S(1)}, u32[]{:S(2)}, u32[]{:S(2)}) collective-permute-start(bf16[256,512]{1,0:T(8,128)(2,1)S(1)} %collective-permute-done.2), channel_id=1, source_target_pairs={{0,2},{2,4},{4,6},{6,8},{8,10},{10,12},{12,14},{14,0},{1,3},{3,5},... | collective-permute-start | bytes 786440 | tf_op jit(solution)/shard_map/ppermute | solution.py:61
  239.1 14.2 %collective-permute-start.4 = (bf16[256,512]{1,0:T(8,128)(2,1)S(1)}, bf16[256,512]{1,0:T(8,128)(2,1)S(1)}, u32[]{:S(2)}, u32[]{:S(2)}) collective-permute-start(bf16[256,512]{1,0:T(8,128)(2,1)S(1)} %collective-permute-done.3), channel_id=1, source_target_pairs={{0,2},{2,4},{4,6},{6,8},{8,10},{10,12},{12,14},{14,0},{1,3},{3,5},... | collective-permute-start | bytes 786440 | tf_op jit(solution)/shard_map/ppermute | solution.py:61
  253.3 15.7 %collective-permute-start.5 = (bf16[256,512]{1,0:T(8,128)(2,1)S(1)}, bf16[256,512]{1,0:T(8,128)(2,1)S(1)}, u32[]{:S(2)}, u32[]{:S(2)}) collective-permute-start(bf16[256,512]{1,0:T(8,128)(2,1)S(1)} %collective-permute-done.4), channel_id=1, source_target_pairs={{0,2},{2,4},{4,6},{6,8},{8,10},{10,12},{12,14},{14,0},{1,3},{3,5},... | collective-permute-start | bytes 786440 | tf_op jit(solution)/shard_map/ppermute | solution.py:61
  269.0 15.7 %collective-permute-start.6 = (bf16[256,512]{1,0:T(8,128)(2,1)S(1)}, bf16[256,512]{1,0:T(8,128)(2,1)S(1)}, u32[]{:S(2)}, u32[]{:S(2)}) collective-permute-start(bf16[256,512]{1,0:T(8,128)(2,1)S(1)} %collective-permute-done.5), channel_id=1, source_target_pairs={{0,2},{2,4},{4,6},{6,8},{8,10},{10,12},{12,14},{14,0},{1,3},{3,5},... | collective-permute-start | bytes 786440 | tf_op jit(solution)/shard_map/ppermute | solution.py:61
  284.7 17.6 %collective-permute-start.7 = (bf16[256,512]{1,0:T(8,128)(2,1)S(1)}, bf16[256,512]{1,0:T(8,128)(2,1)S(1)}, u32[]{:S(2)}, u32[]{:S(2)}) collective-permute-start(bf16[256,512]{1,0:T(8,128)(2,1)S(1)} %collective-permute-done.6), channel_id=1, source_target_pairs={{0,2},{2,4},{4,6},{6,8},{8,10},{10,12},{12,14},{14,0},{1,3},{3,5},... | collective-permute-start | bytes 786440 | tf_op jit(solution)/shard_map/ppermute | solution.py:61
  305.0 21.6 %collective-permute-start.8 = (bf16[256,4096]{1,0:T(8,128)(2,1)S(1)}, bf16[256,4096]{1,0:T(8,128)(2,1)}, u32[]{:S(2)}, u32[]{:S(2)}) collective-permute-start(bf16[256,4096]{1,0:T(8,128)(2,1)S(1)} %constant_dynamic-slice_fusion), channel_id=1, source_target_pairs={{0,16},{16,0},{1,17},{17,1},{2,18},{18,2},{3,19},{19,3},{4,20},{20... | collective-permute-start | bytes 6291464 | tf_op jit(solution)/shard_map/ppermute | solution.py:67
  306.1 20.3 %collective-permute-start.9 = (bf16[2,512,512]{2,1,0:T(8,128)(2,1)}, bf16[2,512,512]{2,1,0:T(8,128)(2,1)}, u32[]{:S(2)}, u32[]{:S(2)}) collective-permute-start(bf16[2,512,512]{2,1,0:T(8,128)(2,1)} %pad_maximum_fusion.6), channel_id=1, source_target_pairs={{0,1},{17,16},{2,3},{19,18},{4,5},{21,20},{6,7},{23,22},{8,9},{25,... | collective-permute-start | bytes 3145736 | tf_op jit(solution)/shard_map/ppermute | solution.py:56
  317.1 114.8 %collective-permute-start.10 = (bf16[4096,512]{1,0:T(8,128)(2,1)}, bf16[4096,512]{1,0:T(8,128)(2,1)}, u32[]{:S(2)}, u32[]{:S(2)}) collective-permute-start(bf16[4096,512]{1,0:T(8,128)(2,1)} %convert_element_type.57), channel_id=1, source_target_pairs={{0,1},{1,0},{2,3},{3,2},{4,5},{5,4},{6,7},{7,6},{8,9},{9,8},{10,11... | collective-permute-start | bytes 12582920 | tf_op jit(solution)/shard_map/ppermute | solution.py:22
  326.6 13.0 %slice-start = ((s8[8388608]{0:T(1024)(128)(4,1)}), s8[4194304]{0:T(1024)(128)(4,1)S(1)}, s32[]{:S(2)}) async-start(s8[8388608]{0:T(1024)(128)(4,1)} %bitcast.59), calls=%async_computation.6 | async-start | bytes 8388608
  329.8 19.7 %copy-start.2 = (bf16[256,4096]{1,0:T(8,128)(2,1)}, bf16[256,4096]{1,0:T(8,128)(2,1)S(1)}, u32[]{:S(2)}) copy-start(bf16[256,4096]{1,0:T(8,128)(2,1)S(1)} %get-tuple-element.22) | copy-start | bytes 6291460
  329.8 9.7 %slice-start.1 = ((s8[8388608]{0:T(1024)(128)(4,1)}), s8[4194304]{0:T(1024)(128)(4,1)S(1)}, s32[]{:S(2)}) async-start(s8[8388608]{0:T(1024)(128)(4,1)} %bitcast.59), calls=%async_computation.7 | async-start | bytes 8388608
  335.2 9.4 %slice-start.2 = ((s8[8388608]{0:T(1024)(128)(4,1)}), s8[4194304]{0:T(1024)(128)(4,1)S(1)}, s32[]{:S(2)}) async-start(s8[8388608]{0:T(1024)(128)(4,1)} %bitcast.61), calls=%async_computation.8 | async-start | bytes 8388608
  335.2 9.4 %slice-start.3 = ((s8[8388608]{0:T(1024)(128)(4,1)}), s8[4194304]{0:T(1024)(128)(4,1)S(1)}, s32[]{:S(2)}) async-start(s8[8388608]{0:T(1024)(128)(4,1)} %bitcast.61), calls=%async_computation.9 | async-start | bytes 8388608
  335.2 88.1 %collective-permute-start.11 = (bf16[512,512]{1,0:T(8,128)(2,1)S(1)}, bf16[512,512]{1,0:T(8,128)(2,1)S(1)}, u32[]{:S(2)}, u32[]{:S(2)}) collective-permute-start(bf16[512,512]{1,0:T(8,128)(2,1)S(1)} %get-tuple-element.27), channel_id=1, source_target_pairs={{0,1},{1,0},{2,3},{3,2},{4,5},{5,4},{6,7},{7,6},{8,9},{9,8},{10,11... | collective-permute-start | bytes 1572872 | tf_op jit(solution)/shard_map/ppermute | solution.py:22
  423.5 9.4 %copy-start.25 = (bf16[1024,8192]{1,0:T(8,128)(2,1)S(1)}, bf16[1024,8192]{1,0:T(8,128)(2,1)}, u32[]{:S(2)}) copy-start(bf16[1024,8192]{1,0:T(8,128)(2,1)} %all-gather.7.cloned.1.call-done) | copy-start | bytes 50331652
  431.8 7.6 %copy-start.13 = (bf16[512,1024]{1,0:T(8,128)(2,1)S(1)}, bf16[512,1024]{1,0:T(8,128)(2,1)}, u32[]{:S(2)}) copy-start(bf16[512,1024]{1,0:T(8,128)(2,1)} %get-tuple-element.18) | copy-start | bytes 3145732
  444.8 217.3 %collective-permute-start.13 = (bf16[1024,512]{1,0:T(8,128)(2,1)}, bf16[1024,512]{1,0:T(8,128)(2,1)}, u32[]{:S(2)}, u32[]{:S(2)}) collective-permute-start(bf16[1024,512]{1,0:T(8,128)(2,1)} %get-tuple-element.33), channel_id=1, source_target_pairs={{0,1},{1,0},{2,3},{3,2},{4,5},{5,4},{6,7},{7,6},{8,9},{9,8},{10,11... | collective-permute-start | bytes 3145736 | tf_op jit(solution)/shard_map/ppermute | solution.py:22
  447.2 9.6 %copy-start.24 = (bf16[1024,8192]{1,0:T(8,128)(2,1)S(1)}, bf16[1024,8192]{1,0:T(8,128)(2,1)}, u32[]{:S(2)}) copy-start(bf16[1024,8192]{1,0:T(8,128)(2,1)} %all-gather.9.cloned.1.call-done) | copy-start | bytes 50331652
  468.5 195.0 %collective-permute-start.14 = (bf16[1024,512]{1,0:T(8,128)(2,1)}, bf16[1024,512]{1,0:T(8,128)(2,1)}, u32[]{:S(2)}, u32[]{:S(2)}) collective-permute-start(bf16[1024,512]{1,0:T(8,128)(2,1)} %get-tuple-element.31), channel_id=1, source_target_pairs={{0,1},{1,0},{2,3},{3,2},{4,5},{5,4},{6,7},{7,6},{8,9},{9,8},{10,11... | collective-permute-start | bytes 3145736 | tf_op jit(solution)/shard_map/ppermute | solution.py:22
  470.5 10.2 %copy-start.23 = (bf16[1024,8192]{1,0:T(8,128)(2,1)S(1)}, bf16[1024,8192]{1,0:T(8,128)(2,1)}, u32[]{:S(2)}) copy-start(bf16[1024,8192]{1,0:T(8,128)(2,1)} %all-gather.11.cloned.1.call-done) | copy-start | bytes 50331652
  487.4 9.6 %copy-start.11 = (bf16[512,1024]{1,0:T(8,128)(2,1)S(1)}, bf16[512,1024]{1,0:T(8,128)(2,1)}, u32[]{:S(2)}) copy-start(bf16[512,1024]{1,0:T(8,128)(2,1)} %get-tuple-element.19) | copy-start | bytes 3145732
  492.7 172.1 %collective-permute-start.15 = (bf16[1024,512]{1,0:T(8,128)(2,1)}, bf16[1024,512]{1,0:T(8,128)(2,1)}, u32[]{:S(2)}, u32[]{:S(2)}) collective-permute-start(bf16[1024,512]{1,0:T(8,128)(2,1)} %get-tuple-element.29), channel_id=1, source_target_pairs={{0,1},{1,0},{2,3},{3,2},{4,5},{5,4},{6,7},{7,6},{8,9},{9,8},{10,11... | collective-permute-start | bytes 3145736 | tf_op jit(solution)/shard_map/ppermute | solution.py:22
  601.0 9.4 %copy-start.26 = (bf16[1024,8192]{1,0:T(8,128)(2,1)S(1)}, bf16[1024,8192]{1,0:T(8,128)(2,1)}, u32[]{:S(2)}) copy-start(bf16[1024,8192]{1,0:T(8,128)(2,1)} %all-gather.5.cloned.1.call-done) | copy-start | bytes 50331652
  620.6 54.1 %copy-start.7 = (f32[1024,512]{1,0:T(8,128)}, f32[1024,512]{1,0:T(8,128)S(1)}, u32[]{:S(2)}) copy-start(f32[1024,512]{1,0:T(8,128)S(1)} %get-tuple-element.36) | copy-start | bytes 6291460
  620.6 41.4 %collective-permute-start.12 = (bf16[1024,512]{1,0:T(8,128)(2,1)S(1)}, bf16[1024,512]{1,0:T(8,128)(2,1)S(1)}, u32[]{:S(2)}, u32[]{:S(2)}) collective-permute-start(bf16[1024,512]{1,0:T(8,128)(2,1)S(1)} %get-tuple-element.35), channel_id=1, source_target_pairs={{0,1},{1,0},{2,3},{3,2},{4,5},{5,4},{6,7},{7,6},{8,9},{9,8},{10,11... | collective-permute-start | bytes 3145736 | tf_op jit(solution)/shard_map/ppermute | solution.py:22
  622.9 38.9 %collective-permute-start.16 = (bf16[512,512]{1,0:T(8,128)(2,1)S(1)}, bf16[512,512]{1,0:T(8,128)(2,1)S(1)}, u32[]{:S(2)}, u32[]{:S(2)}) collective-permute-start(bf16[512,512]{1,0:T(8,128)(2,1)S(1)} %get-tuple-element.37), channel_id=1, source_target_pairs={{0,1},{1,0},{2,3},{3,2},{4,5},{5,4},{6,7},{7,6},{8,9},{9,8},{10,11... | collective-permute-start | bytes 1572872 | tf_op jit(solution)/shard_map/ppermute | solution.py:22
  666.0 11.7 %copy-start.22 = (bf16[4096,512]{1,0:T(8,128)(2,1)}, bf16[4096,512]{1,0:T(8,128)(2,1)S(1)}, u32[]{:S(2)}) copy-start(bf16[4096,512]{1,0:T(8,128)(2,1)S(1)} %constant_dynamic-update-slice_fusion.16) | copy-start | bytes 12582916
  677.8 7.1 copy-start.15
  689.1 8.3 %copy-start.5 = (f32[1024,512]{1,0:T(8,128)S(1)}, f32[1024,512]{1,0:T(8,128)}, u32[]{:S(2)}) copy-start(f32[1024,512]{1,0:T(8,128)} %get-tuple-element.32) | copy-start | bytes 6291460
  689.1 8.3 %copy-start.12 = (bf16[512,1024]{1,0:T(8,128)(2,1)S(1)}, bf16[512,1024]{1,0:T(8,128)(2,1)}, u32[]{:S(2)}) copy-start(bf16[512,1024]{1,0:T(8,128)(2,1)} %get-tuple-element.19) | copy-start | bytes 3145732
  689.1 8.3 %copy-start.18 = (f32[1024,512]{1,0:T(8,128)S(1)}, f32[1024,512]{1,0:T(8,128)}, u32[]{:S(2)}) copy-start(f32[1024,512]{1,0:T(8,128)} %fusion.15) | copy-start | bytes 6291460
  701.1 8.3 %copy-start.6 = (f32[1024,512]{1,0:T(8,128)S(1)}, f32[1024,512]{1,0:T(8,128)}, u32[]{:S(2)}) copy-start(f32[1024,512]{1,0:T(8,128)} %get-tuple-element.30) | copy-start | bytes 6291460
  701.1 8.3 %copy-start.9 = (bf16[512,1024]{1,0:T(8,128)(2,1)S(1)}, bf16[512,1024]{1,0:T(8,128)(2,1)}, u32[]{:S(2)}) copy-start(bf16[512,1024]{1,0:T(8,128)(2,1)} %get-tuple-element.20) | copy-start | bytes 3145732
  701.2 8.3 %copy-start.17 = (f32[1024,512]{1,0:T(8,128)S(1)}, f32[1024,512]{1,0:T(8,128)}, u32[]{:S(2)}) copy-start(f32[1024,512]{1,0:T(8,128)} %fusion.7) | copy-start | bytes 6291460
  715.7 1.1 collective-permute-start.17
  716.9 3.5 collective-permute-start.18
  720.5 3.5 collective-permute-start.19
  724.1 3.5 collective-permute-start.20
  727.6 4.4 collective-permute-start.21
  734.0 14.1 %copy-start.1 = (bf16[1,512,1024]{2,1,0:T(8,128)(2,1)S(1)}, bf16[1,512,1024]{2,1,0:T(8,128)(2,1)}, u32[]{:S(2)}) copy-start(bf16[1,512,1024]{2,1,0:T(8,128)(2,1)} %param.6) | copy-start | bytes 3145732
  (10 other events, 52.3 us)
Sparse Core Ops, SparseCore 0:
  18.8 168.0 reduce-scatter.1
Sparse Core Ops, SparseCore 1:
  24.8 147.7 all-gather.6
  174.7 163.5 all-gather.8
  340.4 130.0 all-gather.10
  472.8 128.1 all-gather.4
